TPU v7x, 32 devices: a whole 2x2x4 slice. The times are simulated.
32 devices in a mesh: gx: 4 (over z), gy: 2 (over x), gz: 4 (over y, core).
Axes of the slice: x: 2, y: 2, z: 4, core: 2. Of those that a mesh axis runs over, the one named last changes fastest.
Arguments:
- positions: bfloat16 [4, 2, 4, 3, 64], P('gx', 'gy', 'gz'), may hold values from 0 to 2
- features: bfloat16 [4, 2, 4, 64, 512], P('gx', 'gy', 'gz'), may hold values from -6 to 6
- ghost_lists: int32 [4, 2, 4, 3, 2, 48], P('gx', 'gy', 'gz'), may hold values from 0 to 63, as said below
- move_lists: int32 [4, 2, 4, 3, 2, 4], P('gx', 'gy', 'gz'), may hold values from 0 to 63, as said below
- neighbours: int32 [4, 2, 4, 8, 64], P('gx', 'gy', 'gz'), may hold values from 0 to 351, as said below
- w_self: bfloat16 [512, 512], replicated, may hold values from -0.25 to 0.25
- w_pair: bfloat16 [512, 512], replicated, may hold values from -0.25 to 0.25
- w_radial: float32 [8, 512], replicated, may hold values from -2 to 2
- w_mix: bfloat16 [512, 512], replicated, may hold values from -0.25 to 0.25
- w_env: bfloat16 [512, 32], replicated, may hold values from -0.25 to 0.25
- w_scal: float32 [96, 512], replicated, may hold values from -0.625 to 0.625
- w_upd: bfloat16 [512, 512], replicated, may hold values from -0.25 to 0.25
- w_out: float32 [512], replicated, may hold values from -0.25 to 0.25
Outputs:
- forces: float32 [4, 2, 4, 3, 64], P('gx', 'gy', 'gz')
- atom_energy: float32 [4, 2, 4, 64], P('gx', 'gy', 'gz')
- moved_positions: bfloat16 [4, 2, 4, 3, 64], P('gx', 'gy', 'gz')
- moved_features: bfloat16 [4, 2, 4, 64, 512], P('gx', 'gy', 'gz')
Inputs may be any that keep to these rules, and one draw needn't show every extreme that they name: `ghost_lists`: each block of 48 entries names distinct atoms. `move_lists`: the 24 entries of one cell are distinct. `neighbours`: entry k of atom i never equals i.
All inputs are finite; a program needn't handle non-finite values.
Results may differ from a plain program's by a relative error of at most 0.015.
Values may be sent and summed in bfloat16 or wider, within the bound.
A program may use at most 64 MiB of HBM per device.

v0:
```python
import math

import jax
import jax.numpy as jnp
from jax import lax
from jax.sharding import PartitionSpec as P

cell_edge = 2.0
basis_width = 0.5


def extended(shard, sides, width):
    for axis, dim in sides:
        size, length = (lax.axis_size(axis), shard.shape[dim])
        up = [(i, (i + 1) % size) for i in range(size)]
        down = [(j, i) for i, j in up]
        last = lax.slice_in_dim(shard, length - width, length, axis=dim)
        initial = lax.slice_in_dim(shard, 0, width, axis=dim)
        before = lax.ppermute(last, axis, up)
        after = lax.ppermute(initial, axis, down)
        shard = jnp.concatenate([before, shard, after], axis=dim)
    return shard


def harmonics(unit_vec):
    ux, uy, uz = (unit_vec[0], unit_vec[1], unit_vec[2])
    root3 = math.sqrt(3.0)
    root15 = math.sqrt(15.0)
    root5 = math.sqrt(5.0)
    return jnp.stack(
        [
            jnp.ones_like(ux),
            root3 * ux,
            root3 * uy,
            root3 * uz,
            root15 * ux * uy,
            root15 * uy * uz,
            0.5 * root5 * (3.0 * uz * uz - 1.0),
            root15 * ux * uz,
            0.5 * root15 * (ux * ux - uy * uy),
        ]
    )


def cell_energy(
    ext_pos, self_proj, ext_pair, neigh_index, w_radial, w_mix, w_env, w_scal, w_upd, w_out
):
    neigh_count, atom_count = neigh_index.shape
    flat_index = neigh_index.T.reshape(-1)
    centre = jnp.repeat(ext_pos[:, :atom_count], neigh_count, axis=1)
    offset = ext_pos[:, flat_index] - centre
    distance = jnp.sqrt(jnp.sum(offset * offset, axis=0) + 0.25)
    harm = harmonics(offset / distance).T
    centers = basis_width * jnp.arange(w_radial.shape[0]).astype(jnp.float32)
    basis = jnp.exp(-jnp.square((distance[:, None] - centers[None, :]) / basis_width))
    before = jnp.repeat(self_proj, neigh_count, axis=0).astype(jnp.float32) + ext_pair[
        flat_index
    ].astype(jnp.float32)
    before = before + jnp.dot(basis, w_radial, precision=lax.Precision.HIGHEST)
    latent = jax.nn.silu(before).astype(jnp.bfloat16)
    mixed = jax.nn.silu(jnp.dot(latent, w_mix, preferred_element_type=jnp.float32)).astype(
        jnp.bfloat16
    )
    env_w = jnp.dot(mixed, w_env, preferred_element_type=jnp.float32)
    channels = env_w.shape[1]
    tensor = env_w[:, :, None] * harm[:, None, :]
    environment = tensor.reshape(atom_count, neigh_count, channels, 9).sum(axis=1) / math.sqrt(
        neigh_count
    )
    project = jnp.repeat(environment, neigh_count, axis=0) * harm[:, None, :]
    invariants = jnp.concatenate(
        [
            project[:, :, 0:1],
            jnp.sum(project[:, :, 1:4], axis=2, keepdims=True),
            jnp.sum(project[:, :, 4:9], axis=2, keepdims=True),
        ],
        axis=2,
    )
    invariants = invariants.reshape(atom_count * neigh_count, 3 * channels)
    update = jax.nn.silu(
        jnp.dot(mixed, w_upd, preferred_element_type=jnp.float32)
        + jnp.dot(invariants, w_scal, precision=lax.Precision.HIGHEST)
    )
    edge_energy = jnp.dot(update, w_out, precision=lax.Precision.HIGHEST)
    return edge_energy.reshape(atom_count, neigh_count).sum(axis=1)


def shards(
    positions,
    features,
    ghost_lists,
    move_lists,
    neighbours,
    w_self,
    w_pair,
    w_radial,
    w_mix,
    w_env,
    w_scal,
    w_upd,
    w_out,
):
    atom_count = positions.shape[-1]
    width = features.shape[-1]
    places16 = positions.reshape(3, atom_count)
    feat_rows = features.reshape(atom_count, width)
    ghost_idx = ghost_lists.reshape(3, 2, -1)
    move_idx = move_lists.reshape(3, 2, -1)
    neigh_index = neighbours.reshape(-1, atom_count)
    ghost_count = ghost_idx.shape[-1]
    self_proj = jnp.dot(feat_rows, w_self, preferred_element_type=jnp.float32).astype(jnp.bfloat16)

    def pack_side(ghost_sel, move_sel):
        ghost_part = jnp.concatenate([feat_rows[ghost_sel], places16[:, ghost_sel].T], axis=1)
        move_part = jnp.concatenate([feat_rows[move_sel], places16[:, move_sel].T], axis=1)
        return jnp.concatenate([ghost_part, move_part], axis=0)

    def outgoing(direction):
        return jnp.stack(
            [
                pack_side(ghost_idx[direction, 0], move_idx[direction, 0]),
                pack_side(ghost_idx[direction, 1], move_idx[direction, 1]),
            ]
        )

    got_x = extended(outgoing(0), (("gx", 0),), 1)
    got_y = extended(outgoing(1), (("gy", 0),), 1)
    got_z = extended(outgoing(2), (("gz", 0),), 1)
    arrivals = (got_x, got_y, got_z)
    places = places16.astype(jnp.float32)
    pos_parts = [places]
    row_parts = [feat_rows]
    shifts = []
    for direction in range(3):
        shift = (jnp.arange(3) == direction).astype(jnp.float32)[:, None] * cell_edge
        shifts.append(shift)
        arrived = arrivals[direction]
        pos_parts.append(arrived[0, :ghost_count, width:].T.astype(jnp.float32) - shift)
        pos_parts.append(arrived[3, :ghost_count, width:].T.astype(jnp.float32) + shift)
        row_parts.append(arrived[0, :ghost_count, :width])
        row_parts.append(arrived[3, :ghost_count, :width])
    ext_pos = jnp.concatenate(pos_parts, axis=1)
    ext_rows = jnp.concatenate(row_parts, axis=0)
    ext_pair = jnp.dot(ext_rows, w_pair, preferred_element_type=jnp.float32).astype(jnp.bfloat16)

    def energy_of(coords):
        return cell_energy(
            coords, self_proj, ext_pair, neigh_index, w_radial, w_mix, w_env, w_scal, w_upd, w_out
        )

    energy, pullback = jax.vjp(energy_of, ext_pos)
    gradient = pullback(jnp.ones_like(energy))[0]
    forces = -gradient[:, :atom_count]

    def ghost_block(direction, side):
        start = atom_count + (2 * direction + side) * ghost_count
        return gradient[:, start : start + ghost_count]

    back_x = extended(jnp.stack([ghost_block(0, 0), ghost_block(0, 1)]), (("gx", 0),), 1)
    back_y = extended(jnp.stack([ghost_block(1, 0), ghost_block(1, 1)]), (("gy", 0),), 1)
    back_z = extended(jnp.stack([ghost_block(2, 0), ghost_block(2, 1)]), (("gz", 0),), 1)
    returned = (back_x, back_y, back_z)
    for direction in range(3):
        forces = forces.at[:, ghost_idx[direction, 0]].add(-returned[direction][0])
        forces = forces.at[:, ghost_idx[direction, 1]].add(-returned[direction][3])
    moved_pos = places
    moved_feat = feat_rows
    for direction in range(3):
        arrived = arrivals[direction]
        moved_pos = moved_pos.at[:, move_idx[direction, 0]].set(
            arrived[0, ghost_count:, width:].T.astype(jnp.float32) - shifts[direction]
        )
        moved_pos = moved_pos.at[:, move_idx[direction, 1]].set(
            arrived[3, ghost_count:, width:].T.astype(jnp.float32) + shifts[direction]
        )
        moved_feat = moved_feat.at[move_idx[direction, 0]].set(arrived[0, ghost_count:, :width])
        moved_feat = moved_feat.at[move_idx[direction, 1]].set(arrived[3, ghost_count:, :width])
    return (
        forces.reshape(1, 1, 1, 3, atom_count),
        energy.reshape(1, 1, 1, atom_count),
        moved_pos.astype(jnp.bfloat16).reshape(1, 1, 1, 3, atom_count),
        moved_feat.reshape(1, 1, 1, atom_count, width),
    )


def solution(mesh):
    placed = (
        P("gx", "gy", "gz", None, None),
        P("gx", "gy", "gz", None, None),
        P("gx", "gy", "gz", None, None, None),
        P("gx", "gy", "gz", None, None, None),
        P("gx", "gy", "gz", None, None),
        P(),
        P(),
        P(),
        P(),
        P(),
        P(),
        P(),
        P(),
    )
    return jax.shard_map(
        shards,
        mesh=mesh,
        in_specs=placed,
        out_specs=(
            P("gx", "gy", "gz", None, None),
            P("gx", "gy", "gz", None),
            P("gx", "gy", "gz", None, None),
            P("gx", "gy", "gz", None, None),
        ),
        check_vma=False,
    )
```

profile of v0, /device:TPU:0, one launch (start us, length us, event | category | flops | bytes accessed | tf_op | source)
XLA Modules:
  0.0 85.6 jit_solution(17302130515149362214)
XLA Ops:
  0.7 0.9 %copy.301 = bf16[1,1,1,64,512]{4,3,2,1,0:T(8,128)(2,1)S(1)} copy(bf16[1,1,1,64,512]{4,3,2,1,0:T(8,128)(2,1)} %param.14) | data formatting | bytes 131072
  6.4 3.1 %collective-permute-start = (bf16[1,52,515]{2,1,0:T(8,128)(2,1)S(1)}, bf16[1,52,515]{2,1,0:T(8,128)(2,1)S(1)}, u32[]{:S(2)}, u32[]{:S(2)}) collective-permute-start(bf16[1,52,515]{2,1,0:T(8,128)(2,1)S(1)} %maximum_bitcast_fusion), channel_id=1, source_target_pairs={{0,8},{8,16},{16,24},{24,0},{1,9},{9,17},{17,25},{25,1},{2,10},{10... | collective-permute-start | bytes 160688 | tf_op jit(solution)/shard_map/ppermute | solution.py:19
  11.9 2.1 %collective-permute-start.1 = (bf16[1,52,515]{2,1,0:T(8,128)(2,1)S(1)}, bf16[1,52,515]{2,1,0:T(8,128)(2,1)S(1)}, u32[]{:S(2)}, u32[]{:S(2)}) collective-permute-start(bf16[1,52,515]{2,1,0:T(8,128)(2,1)S(1)} %maximum_bitcast_fusion.1), channel_id=1, source_target_pairs={{8,0},{16,8},{24,16},{0,24},{9,1},{17,9},{25,17},{1,25},{10,2},{18... | collective-permute-start | bytes 160688 | tf_op jit(solution)/shard_map/ppermute | solution.py:20
  16.5 1.8 %collective-permute-start.2 = (bf16[1,52,515]{2,1,0:T(8,128)(2,1)S(1)}, bf16[1,52,515]{2,1,0:T(8,128)(2,1)S(1)}, u32[]{:S(2)}, u32[]{:S(2)}) collective-permute-start(bf16[1,52,515]{2,1,0:T(8,128)(2,1)S(1)} %maximum_bitcast_fusion.2), channel_id=1, source_target_pairs={{0,4},{4,0},{1,5},{5,1},{2,6},{6,2},{3,7},{7,3},{8,12},{12,8},{9,1... | collective-permute-start | bytes 160688 | tf_op jit(solution)/shard_map/ppermute | solution.py:19
  26.9 1.9 %collective-permute-start.5 = (bf16[1,52,515]{2,1,0:T(8,128)(2,1)S(1)}, bf16[1,52,515]{2,1,0:T(8,128)(2,1)S(1)}, u32[]{:S(2)}, u32[]{:S(2)}) collective-permute-start(bf16[1,52,515]{2,1,0:T(8,128)(2,1)S(1)} %maximum_bitcast_fusion.5), channel_id=1, source_target_pairs={{1,0},{2,1},{3,2},{0,3},{5,4},{6,5},{7,6},{4,7},{9,8},{10,9},{11,1... | collective-permute-start | bytes 160688 | tf_op jit(solution)/shard_map/ppermute | solution.py:20
  29.0 1.8 %collective-permute-done.5 = bf16[1,52,515]{2,1,0:T(8,128)(2,1)S(1)} collective-permute-done((bf16[1,52,515]{2,1,0:T(8,128)(2,1)S(1)}, bf16[1,52,515]{2,1,0:T(8,128)(2,1)S(1)}, u32[]{:S(2)}, u32[]{:S(2)}) %collective-permute-start.5) | collective-permute-done | bytes 53592 | tf_op jit(solution)/shard_map/ppermute | solution.py:20
  30.8 1.0 %gather_fusion.24 = f32[512,3]{1,0:T(8,128)S(1)} fusion(f32[3,352]{0,1:T(8,128)S(1)} %constant_dynamic-update-slice_fusion, s32[1024]{0:T(1024)S(1)} %pad_clamp_fusion), kind=kCustom, calls=%fused_computation.24 | custom fusion | bytes 14336 | tf_op jit(solution)/shard_map/jvp()/gather | solution.py:51
  33.0 2.0 %gather_fusion.25 = bf16[512,512]{1,0:T(8,128)(2,1)S(1)} fusion(bf16[352,512]{1,0:T(8,128)(2,1)S(1)} %convolution_convert_fusion.3, s32[1024]{0:T(1024)S(1)} %pad_clamp_fusion), kind=kCustom, calls=%fused_computation.25 | custom fusion | bytes 1050624 | tf_op jit(solution)/shard_map/jvp()/gather | solution.py:56
  35.0 1.1 %convolution_add_fusion.1 = f32[512,512]{1,0:T(8,128)S(1)} fusion(f32[8,512]{1,0:T(8,128)S(1)} %copy-done.15, bf16[512,512]{1,0:T(8,128)(2,1)S(1)} %gather_fusion.25, f32[64,512]{1,0:T(8,128)S(1)} %fusion.2, f32[8]{0:T(128)S(1)} %convert_multiply_fusion.4, f32[512]{0:T(512)S(1)} %get-tuple-element.86), kind=kOutput, calls=%fused_computation.54 | convolution fusion | flops 25968640 | bytes 1722400 | tf_op jit(solution)/shard_map/jvp()/dot_general | solution.py:59
  36.2 1.6 %multiply_convert_fusion = (bf16[512,512]{1,0:T(8,128)(2,1)S(1)}, f32[512,512]{1,0:T(8,128)}) fusion(bf16[512,512]{1,0:T(8,128)(2,1)S(1)} %copy-done, f32[512,512]{1,0:T(8,128)S(1)} %convolution_add_fusion.1), kind=kOutput, calls=%fused_computation.86 | convolution fusion | flops 271056896 | bytes 3145728 | tf_op jit(solution)/shard_map/jvp()/dot_general | solution.py:61
  40.2 1.0 %fusion.114 = f32[512,512]{1,0:T(8,128)S(1)} fusion(f32[512,96]{0,1:T(8,128)S(1)} %reshape.553, f32[96,512]{1,0:T(8,128)S(1)} %copy-done.7), kind=kOutput, calls=%fused_computation.313 | convolution fusion | flops 301989888 | bytes 1441792 | tf_op jit(solution)/shard_map/jvp()/dot_general | solution.py:82
  41.7 1.5 %fusion.110 = f32[512,96]{0,1:T(8,128)S(1)} fusion(f32[96,512]{1,0:T(8,128)S(1)} %copy-done.7, f32[512,512]{1,0:T(8,128)S(1)} %convolution_add_fusion, f32[512]{0:T(512)S(1)} %copy-done.26), kind=kOutput, calls=%fused_computation.310 | convolution fusion | flops 304349184 | bytes 1443840 | tf_op jit(solution)/shard_map/transpose(jvp())/dot_general | solution.py:82
  44.8 3.3 %bitcast_reduce_fusion = f32[64,32,9]{1,0,2:T(8,128)S(1)} fusion(f32[512,32,1]{1,0,2:T(8,128)S(1)} %copy.268, f32[512,32,3]{1,0,2:T(8,128)S(1)} %broadcast_in_dim.24, f32[512,32,5]{1,0,2:T(8,128)S(1)} %broadcast_in_dim.23, f32[512,9]{0,1:T(8,128)S(1)} %bitcast.374), kind=kLoop, calls=%fused_computation.48 | loop fusion | flops 571392 | bytes 681984 | tf_op jit(solution)/shard_map/transpose(jvp())/reduce_sum | solution.py:70
  49.4 3.4 %convolution_convert_fusion = bf16[512,512]{1,0:T(8,128)(2,1)} fusion(bf16[512,512]{1,0:T(8,128)(2,1)S(1)} %copy-done, f32[512,512]{1,0:T(8,128)} %get-tuple-element.88, bf16[512,512]{1,0:T(8,128)(2,1)S(1)} %convolution_convert_fusion.2, bf16[512,512]{1,0:T(8,128)(2,1)} %param.24, f32[512,512]{1,0:T(8,128)S(1)} %convolution_add_fusion, f32[512]{0:T(512)S(1)} %copy-done.27), kind=kOutput, calls=%fused_computation.60 | convolution fusion | flops 542638080 | bytes 4196352 | tf_op jit(solution)/shard_map/transpose(jvp())/dot_general | solution.py:61
  52.8 2.5 %fusion.6 = f32[512]{0:T(512)S(1)} fusion(f32[8,512]{1,0:T(8,128)S(1)} %copy-done.15, bf16[512,512]{1,0:T(8,128)(2,1)} %convolution_convert_fusion, f32[512,512]{1,0:T(8,128)S(1)} %copy-done.3, f32[8]{0:T(128)S(1)} %copy-done.25, f32[512]{0:T(512)S(1)} %get-tuple-element.86), kind=kOutput, calls=%fused_computation.75 | convolution fusion | flops 27827712 | bytes 1593376 | tf_op jit(solution)/shard_map/transpose(jvp())/dot_general | solution.py:59
  55.9 3.3 %scatter_fusion = f32[3,352]{0,1:T(8,128)S(1)} fusion(f32[3,352]{0,1:T(8,128)S(1)} %pad.27, s32[512]{0:T(512)S(1)} %bitcast.378, f32[512,3]{1,0:T(8,128)S(1)} %copy.262), kind=kCustom, calls=%fused_computation.26 | custom fusion | flops 1536 | bytes 20480 | tf_op jit(solution)/shard_map/transpose(jvp())/scatter-add | solution.py:51
  64.8 1.2 %fusion.17 = f32[1,512]{1,0:T(1,128)S(1)} fusion(f32[512,1]{0,1:T(1,128)S(1)} %bitcast.384, f32[512,512]{1,0:T(8,128)S(1)} %convolution_add_fusion), kind=kOutput, calls=%fused_computation.83 | convolution fusion | flops 4194304 | bytes 1052672 | tf_op jit(solution)/shard_map/jvp()/dot_general | solution.py:84
  66.8 1.9 %collective-permute-start.10 = (f32[1,3,48]{1,2,0:T(8,128)S(1)}, f32[1,3,48]{1,2,0:T(8,128)S(1)}, u32[]{:S(2)}, u32[]{:S(2)}) collective-permute-start(f32[1,3,48]{1,2,0:T(8,128)S(1)} %get-tuple-element.58), channel_id=1, source_target_pairs={{0,1},{1,2},{2,3},{3,0},{4,5},{5,6},{6,7},{7,4},{8,9},{9,10},{10,1... | collective-permute-start | bytes 1736 | tf_op jit(solution)/shard_map/ppermute | solution.py:19
  68.6 1.5 %collective-permute-start.9 = (f32[1,3,48]{1,2,0:T(8,128)S(1)}, f32[1,3,48]{1,2,0:T(8,128)S(1)}, u32[]{:S(2)}, u32[]{:S(2)}) collective-permute-start(f32[1,3,48]{1,2,0:T(8,128)S(1)} %get-tuple-element.59), channel_id=1, source_target_pairs={{4,0},{0,4},{5,1},{1,5},{6,2},{2,6},{7,3},{3,7},{12,8},{8,12},{13,... | collective-permute-start | bytes 1736 | tf_op jit(solution)/shard_map/ppermute | solution.py:20
  70.1 3.5 %collective-permute-start.7 = (f32[1,3,48]{1,2,0:T(8,128)S(1)}, f32[1,3,48]{1,2,0:T(8,128)S(1)}, u32[]{:S(2)}, u32[]{:S(2)}) collective-permute-start(f32[1,3,48]{1,2,0:T(8,128)S(1)} %get-tuple-element.61), channel_id=1, source_target_pairs={{8,0},{16,8},{24,16},{0,24},{9,1},{17,9},{25,17},{1,25},{10,2},{18... | collective-permute-start | bytes 1736 | tf_op jit(solution)/shard_map/ppermute | solution.py:20
  74.2 0.8 scatter_custom_fusion.13
  75.1 0.9 %scatter_custom_fusion.14 = bf16[64,512]{1,0:T(8,128)(2,1)S(1)} fusion(bf16[64,512]{1,0:T(8,128)(2,1)S(1)} %scatter_custom_fusion.13, s32[4]{0:T(128)} %copy-done.22, bf16[1,52,515]{2,1,0:T(8,128)(2,1)} %copy-done.10), kind=kCustom, calls=%fused_computation.193 | custom fusion | bytes 69632 | tf_op jit(solution)/shard_map/scatter | solution.py:177
  75.9 0.9 %scatter_custom_fusion.15 = bf16[64,512]{1,0:T(8,128)(2,1)S(1)} fusion(bf16[64,512]{1,0:T(8,128)(2,1)S(1)} %scatter_custom_fusion.14, s32[4]{0:T(128)} %copy-done.21, bf16[1,52,515]{2,1,0:T(8,128)(2,1)} %copy-done.11), kind=kCustom, calls=%fused_computation.191 | custom fusion | bytes 69632 | tf_op jit(solution)/shard_map/scatter | solution.py:176
  76.8 0.9 %scatter_custom_fusion.16 = bf16[64,512]{1,0:T(8,128)(2,1)S(1)} fusion(bf16[64,512]{1,0:T(8,128)(2,1)S(1)} %scatter_custom_fusion.15, s32[4]{0:T(128)} %copy-done.20, bf16[1,52,515]{2,1,0:T(8,128)(2,1)} %copy-done.12), kind=kCustom, calls=%fused_computation.189 | custom fusion | bytes 69632 | tf_op jit(solution)/shard_map/scatter | solution.py:177
  77.7 0.9 %scatter_custom_fusion.17 = bf16[64,512]{1,0:T(8,128)(2,1)S(1)} fusion(bf16[64,512]{1,0:T(8,128)(2,1)S(1)} %scatter_custom_fusion.16, s32[4]{0:T(128)} %copy-done.19, bf16[1,52,515]{2,1,0:T(8,128)(2,1)} %copy-done.13), kind=kCustom, calls=%fused_computation.187 | custom fusion | bytes 69632 | tf_op jit(solution)/shard_map/scatter | solution.py:176
  78.6 0.9 %scatter_custom_fusion.18 = bf16[64,512]{1,0:T(8,128)(2,1)S(1)} fusion(bf16[64,512]{1,0:T(8,128)(2,1)S(1)} %scatter_custom_fusion.17, s32[4]{0:T(128)} %copy-done.18, bf16[1,52,515]{2,1,0:T(8,128)(2,1)} %copy-done.14), kind=kCustom, calls=%fused_computation.185 | custom fusion | bytes 69632 | tf_op jit(solution)/shard_map/scatter | solution.py:177
  79.5 1.0 %scatter_custom_fusion.1 = f32[3,64]{0,1:T(8,128)S(1)} fusion(f32[3,64]{0,1:T(8,128)S(1)} %slice_negate_fusion, s32[48]{0:T(128)} %copy-done.17, f32[1,3,48]{1,2,0:T(8,128)S(1)} %collective-permute-done.6), kind=kCustom, calls=%fused_computation.143 | custom fusion | flops 288 | bytes 25344 | tf_op jit(solution)/shard_map/scatter-add | solution.py:164
  80.5 0.9 %scatter_custom_fusion.2 = f32[3,64]{0,1:T(8,128)S(1)} fusion(f32[3,64]{0,1:T(8,128)S(1)} %scatter_custom_fusion.1, s32[48]{0:T(128)S(1)} %get-tuple-element.78, f32[1,3,48]{1,2,0:T(8,128)S(1)} %collective-permute-done.7), kind=kCustom, calls=%fused_computation.141 | custom fusion | flops 288 | bytes 25344 | tf_op jit(solution)/shard_map/scatter-add | solution.py:165
  81.4 0.9 %scatter_custom_fusion.3 = f32[3,64]{0,1:T(8,128)S(1)} fusion(f32[3,64]{0,1:T(8,128)S(1)} %scatter_custom_fusion.2, s32[48]{0:T(128)S(1)} %get-tuple-element.75, f32[1,3,48]{1,2,0:T(8,128)S(1)} %collective-permute-done.8), kind=kCustom, calls=%fused_computation.139 | custom fusion | flops 288 | bytes 25344 | tf_op jit(solution)/shard_map/scatter-add | solution.py:164
  82.3 0.9 %scatter_custom_fusion.4 = f32[3,64]{0,1:T(8,128)S(1)} fusion(f32[3,64]{0,1:T(8,128)S(1)} %scatter_custom_fusion.3, s32[48]{0:T(128)S(1)} %get-tuple-element.76, f32[1,3,48]{1,2,0:T(8,128)S(1)} %collective-permute-done.9), kind=kCustom, calls=%fused_computation.137 | custom fusion | flops 288 | bytes 25344 | tf_op jit(solution)/shard_map/scatter-add | solution.py:165
  83.2 0.9 %scatter_custom_fusion.5 = f32[3,64]{0,1:T(8,128)S(1)} fusion(f32[3,64]{0,1:T(8,128)S(1)} %scatter_custom_fusion.4, s32[48]{0:T(128)S(1)} %get-tuple-element.73, f32[1,3,48]{1,2,0:T(8,128)S(1)} %collective-permute-done.10), kind=kCustom, calls=%fused_computation.135 | custom fusion | flops 288 | bytes 25344 | tf_op jit(solution)/shard_map/scatter-add | solution.py:164
  84.1 0.9 %scatter_custom_fusion.6 = f32[3,64]{0,1:T(8,128)S(1)} fusion(f32[3,64]{0,1:T(8,128)S(1)} %scatter_custom_fusion.5, s32[48]{0:T(128)S(1)} %get-tuple-element.74, f32[1,3,48]{1,2,0:T(8,128)S(1)} %collective-permute-done.11), kind=kCustom, calls=%fused_computation.133 | custom fusion | flops 288 | bytes 25344 | tf_op jit(solution)/shard_map/scatter-add | solution.py:165
  (200 shorter events, 32.7 us)
Async XLA Ops:
  0.6 35.5 %copy-start = (bf16[512,512]{1,0:T(8,128)(2,1)S(1)}, bf16[512,512]{1,0:T(8,128)(2,1)}, u32[]{:S(2)}) copy-start(bf16[512,512]{1,0:T(8,128)(2,1)} %param.21) | copy-start | bytes 1572868
  0.6 25.5 %copy-start.16 = (s32[1,1,1,8,64]{4,3,2,1,0:T(8,128)S(1)}, s32[1,1,1,8,64]{4,3,2,1,0:T(8,128)}, u32[]{:S(2)}) copy-start(s32[1,1,1,8,64]{4,3,2,1,0:T(8,128)} %param.17) | copy-start | bytes 6148
  0.7 25.7 %copy-start.4 = (bf16[512,512]{1,0:T(8,128)(2,1)S(1)}, bf16[512,512]{1,0:T(8,128)(2,1)}, u32[]{:S(2)}) copy-start(bf16[512,512]{1,0:T(8,128)(2,1)} %param.18) | copy-start | bytes 1572868
  3.1 20.4 %copy-start.22 = (s32[4]{0:T(128)}, s32[4]{0:T(128)S(1)}, u32[]{:S(2)}) copy-start(s32[4]{0:T(128)S(1)} %get-tuple-element.84) | copy-start | bytes 52
  3.2 20.4 %copy-start.21 = (s32[4]{0:T(128)}, s32[4]{0:T(128)S(1)}, u32[]{:S(2)}) copy-start(s32[4]{0:T(128)S(1)} %get-tuple-element.81) | copy-start | bytes 52
  3.2 20.5 %copy-start.20 = (s32[4]{0:T(128)}, s32[4]{0:T(128)S(1)}, u32[]{:S(2)}) copy-start(s32[4]{0:T(128)S(1)} %get-tuple-element.82) | copy-start | bytes 52
  3.2 23.4 %copy-start.18 = (s32[4]{0:T(128)}, s32[4]{0:T(128)S(1)}, u32[]{:S(2)}) copy-start(s32[4]{0:T(128)S(1)} %get-tuple-element.80) | copy-start | bytes 52
  3.2 23.4 %copy-start.19 = (s32[4]{0:T(128)}, s32[4]{0:T(128)S(1)}, u32[]{:S(2)}) copy-start(s32[4]{0:T(128)S(1)} %get-tuple-element.79) | copy-start | bytes 52
  3.2 23.4 %copy-start.23 = (s32[4]{0:T(128)}, s32[4]{0:T(128)S(1)}, u32[]{:S(2)}) copy-start(s32[4]{0:T(128)S(1)} %get-tuple-element.83) | copy-start | bytes 52
  6.4 20.5 %collective-permute-start = (bf16[1,52,515]{2,1,0:T(8,128)(2,1)S(1)}, bf16[1,52,515]{2,1,0:T(8,128)(2,1)S(1)}, u32[]{:S(2)}, u32[]{:S(2)}) collective-permute-start(bf16[1,52,515]{2,1,0:T(8,128)(2,1)S(1)} %maximum_bitcast_fusion), channel_id=1, source_target_pairs={{0,8},{8,16},{16,24},{24,0},{1,9},{9,17},{17,25},{25,1},{2,10},{10... | collective-permute-start | bytes 160688 | tf_op jit(solution)/shard_map/ppermute | solution.py:19
  11.9 16.9 %collective-permute-start.1 = (bf16[1,52,515]{2,1,0:T(8,128)(2,1)S(1)}, bf16[1,52,515]{2,1,0:T(8,128)(2,1)S(1)}, u32[]{:S(2)}, u32[]{:S(2)}) collective-permute-start(bf16[1,52,515]{2,1,0:T(8,128)(2,1)S(1)} %maximum_bitcast_fusion.1), channel_id=1, source_target_pairs={{8,0},{16,8},{24,16},{0,24},{9,1},{17,9},{25,17},{1,25},{10,2},{18... | collective-permute-start | bytes 160688 | tf_op jit(solution)/shard_map/ppermute | solution.py:20
  16.5 12.4 %collective-permute-start.2 = (bf16[1,52,515]{2,1,0:T(8,128)(2,1)S(1)}, bf16[1,52,515]{2,1,0:T(8,128)(2,1)S(1)}, u32[]{:S(2)}, u32[]{:S(2)}) collective-permute-start(bf16[1,52,515]{2,1,0:T(8,128)(2,1)S(1)} %maximum_bitcast_fusion.2), channel_id=1, source_target_pairs={{0,4},{4,0},{1,5},{5,1},{2,6},{6,2},{3,7},{7,3},{8,12},{12,8},{9,1... | collective-permute-start | bytes 160688 | tf_op jit(solution)/shard_map/ppermute | solution.py:19
  20.7 12.0 %copy-start.5 = (bf16[512,512]{1,0:T(8,128)(2,1)S(1)}, bf16[512,512]{1,0:T(8,128)(2,1)}, u32[]{:S(2)}) copy-start(bf16[512,512]{1,0:T(8,128)(2,1)} %param.19) | copy-start | bytes 1572868
  20.7 8.2 %collective-permute-start.3 = (bf16[1,52,515]{2,1,0:T(8,128)(2,1)S(1)}, bf16[1,52,515]{2,1,0:T(8,128)(2,1)S(1)}, u32[]{:S(2)}, u32[]{:S(2)}) collective-permute-start(bf16[1,52,515]{2,1,0:T(8,128)(2,1)S(1)} %maximum_bitcast_fusion.3), channel_id=1, source_target_pairs={{4,0},{0,4},{5,1},{1,5},{6,2},{2,6},{7,3},{3,7},{12,8},{8,12},{13,... | collective-permute-start | bytes 160688 | tf_op jit(solution)/shard_map/ppermute | solution.py:20
  23.5 5.4 %collective-permute-start.4 = (bf16[1,52,515]{2,1,0:T(8,128)(2,1)S(1)}, bf16[1,52,515]{2,1,0:T(8,128)(2,1)S(1)}, u32[]{:S(2)}, u32[]{:S(2)}) collective-permute-start(bf16[1,52,515]{2,1,0:T(8,128)(2,1)S(1)} %maximum_bitcast_fusion.4), channel_id=1, source_target_pairs={{0,1},{1,2},{2,3},{3,0},{4,5},{5,6},{6,7},{7,4},{8,9},{9,10},{10,1... | collective-permute-start | bytes 160688 | tf_op jit(solution)/shard_map/ppermute | solution.py:19
  26.6 8.4 %copy-start.24 = (f32[8]{0:T(128)}, f32[8]{0:T(128)S(1)}, u32[]{:S(2)}) copy-start(f32[8]{0:T(128)S(1)} %convert_multiply_fusion.4) | copy-start | bytes 100
  26.9 8.1 %copy-start.9 = (bf16[1,52,515]{2,1,0:T(8,128)(2,1)}, bf16[1,52,515]{2,1,0:T(8,128)(2,1)S(1)}, u32[]{:S(2)}) copy-start(bf16[1,52,515]{2,1,0:T(8,128)(2,1)S(1)} %collective-permute-done) | copy-start | bytes 160684
  26.9 3.9 %collective-permute-start.5 = (bf16[1,52,515]{2,1,0:T(8,128)(2,1)S(1)}, bf16[1,52,515]{2,1,0:T(8,128)(2,1)S(1)}, u32[]{:S(2)}, u32[]{:S(2)}) collective-permute-start(bf16[1,52,515]{2,1,0:T(8,128)(2,1)S(1)} %maximum_bitcast_fusion.5), channel_id=1, source_target_pairs={{1,0},{2,1},{3,2},{0,3},{5,4},{6,5},{7,6},{4,7},{9,8},{10,9},{11,1... | collective-permute-start | bytes 160688 | tf_op jit(solution)/shard_map/ppermute | solution.py:20
  28.9 6.1 %copy-start.10 = (bf16[1,52,515]{2,1,0:T(8,128)(2,1)}, bf16[1,52,515]{2,1,0:T(8,128)(2,1)S(1)}, u32[]{:S(2)}) copy-start(bf16[1,52,515]{2,1,0:T(8,128)(2,1)S(1)} %collective-permute-done.1) | copy-start | bytes 160684
  28.9 6.1 %copy-start.11 = (bf16[1,52,515]{2,1,0:T(8,128)(2,1)}, bf16[1,52,515]{2,1,0:T(8,128)(2,1)S(1)}, u32[]{:S(2)}) copy-start(bf16[1,52,515]{2,1,0:T(8,128)(2,1)S(1)} %collective-permute-done.2) | copy-start | bytes 160684
  28.9 6.1 %copy-start.12 = (bf16[1,52,515]{2,1,0:T(8,128)(2,1)}, bf16[1,52,515]{2,1,0:T(8,128)(2,1)S(1)}, u32[]{:S(2)}) copy-start(bf16[1,52,515]{2,1,0:T(8,128)(2,1)S(1)} %collective-permute-done.3) | copy-start | bytes 160684
  29.0 6.0 %copy-start.13 = (bf16[1,52,515]{2,1,0:T(8,128)(2,1)}, bf16[1,52,515]{2,1,0:T(8,128)(2,1)S(1)}, u32[]{:S(2)}) copy-start(bf16[1,52,515]{2,1,0:T(8,128)(2,1)S(1)} %collective-permute-done.4) | copy-start | bytes 160684
  44.8 4.6 %copy-start.27 = (f32[512]{0:T(512)S(1)}, f32[512]{0:T(512)}, u32[]{:S(2)}) copy-start(f32[512]{0:T(512)} %param.25) | copy-start | bytes 6148
  49.4 3.5 %copy-start.3 = (f32[512,512]{1,0:T(8,128)S(1)}, f32[512,512]{1,0:T(8,128)}, u32[]{:S(2)}) copy-start(f32[512,512]{1,0:T(8,128)} %copy-done.2) | copy-start | bytes 3145732
  49.4 3.4 %copy-start.25 = (f32[8]{0:T(128)S(1)}, f32[8]{0:T(128)}, u32[]{:S(2)}) copy-start(f32[8]{0:T(128)} %copy-done.24) | copy-start | bytes 100
  66.8 10.9 %collective-permute-start.6 = (f32[1,3,48]{1,2,0:T(8,128)S(1)}, f32[1,3,48]{1,2,0:T(8,128)S(1)}, u32[]{:S(2)}, u32[]{:S(2)}) collective-permute-start(f32[1,3,48]{1,2,0:T(8,128)S(1)} %get-tuple-element.62), channel_id=1, source_target_pairs={{0,8},{8,16},{16,24},{24,0},{1,9},{9,17},{17,25},{25,1},{2,10},{10... | collective-permute-start | bytes 1736 | tf_op jit(solution)/shard_map/ppermute | solution.py:19
  66.8 16.4 %collective-permute-start.10 = (f32[1,3,48]{1,2,0:T(8,128)S(1)}, f32[1,3,48]{1,2,0:T(8,128)S(1)}, u32[]{:S(2)}, u32[]{:S(2)}) collective-permute-start(f32[1,3,48]{1,2,0:T(8,128)S(1)} %get-tuple-element.58), channel_id=1, source_target_pairs={{0,1},{1,2},{2,3},{3,0},{4,5},{5,6},{6,7},{7,4},{8,9},{9,10},{10,1... | collective-permute-start | bytes 1736 | tf_op jit(solution)/shard_map/ppermute | solution.py:19
  68.6 13.6 %collective-permute-start.9 = (f32[1,3,48]{1,2,0:T(8,128)S(1)}, f32[1,3,48]{1,2,0:T(8,128)S(1)}, u32[]{:S(2)}, u32[]{:S(2)}) collective-permute-start(f32[1,3,48]{1,2,0:T(8,128)S(1)} %get-tuple-element.59), channel_id=1, source_target_pairs={{4,0},{0,4},{5,1},{1,5},{6,2},{2,6},{7,3},{3,7},{12,8},{8,12},{13,... | collective-permute-start | bytes 1736 | tf_op jit(solution)/shard_map/ppermute | solution.py:20
  70.1 10.3 %collective-permute-start.7 = (f32[1,3,48]{1,2,0:T(8,128)S(1)}, f32[1,3,48]{1,2,0:T(8,128)S(1)}, u32[]{:S(2)}, u32[]{:S(2)}) collective-permute-start(f32[1,3,48]{1,2,0:T(8,128)S(1)} %get-tuple-element.61), channel_id=1, source_target_pairs={{8,0},{16,8},{24,16},{0,24},{9,1},{17,9},{25,17},{1,25},{10,2},{18... | collective-permute-start | bytes 1736 | tf_op jit(solution)/shard_map/ppermute | solution.py:20
  73.7 7.7 %collective-permute-start.8 = (f32[1,3,48]{1,2,0:T(8,128)S(1)}, f32[1,3,48]{1,2,0:T(8,128)S(1)}, u32[]{:S(2)}, u32[]{:S(2)}) collective-permute-start(f32[1,3,48]{1,2,0:T(8,128)S(1)} %get-tuple-element.60), channel_id=1, source_target_pairs={{0,4},{4,0},{1,5},{5,1},{2,6},{6,2},{3,7},{7,3},{8,12},{12,8},{9,1... | collective-permute-start | bytes 1736 | tf_op jit(solution)/shard_map/ppermute | solution.py:19
  77.7 6.4 %collective-permute-start.11 = (f32[1,3,48]{1,2,0:T(8,128)S(1)}, f32[1,3,48]{1,2,0:T(8,128)S(1)}, u32[]{:S(2)}, u32[]{:S(2)}) collective-permute-start(f32[1,3,48]{1,2,0:T(8,128)S(1)} %get-tuple-element.57), channel_id=1, source_target_pairs={{1,0},{2,1},{3,2},{0,3},{5,4},{6,5},{7,6},{4,7},{9,8},{10,9},{11,1... | collective-permute-start | bytes 1736 | tf_op jit(solution)/shard_map/ppermute | solution.py:20
  79.5 6.1 %copy-start.1 = (bf16[64,512]{1,0:T(8,128)(2,1)}, bf16[64,512]{1,0:T(8,128)(2,1)S(1)}, u32[]{:S(2)}) copy-start(bf16[64,512]{1,0:T(8,128)(2,1)S(1)} %scatter_custom_fusion.18) | copy-start | bytes 196612
  (8 other events, 14.1 us)
where the time goes:
time: 86.3 us; the launch traced here: 85.6 us
  local copies, waits for them, and re-layouts  29.6 us (34%)
  other arithmetic  21.6 us (25%)
  starting transfers between devices  16.8 us (19%)
  matrix products  13.8 us (16%)
  between operations  1.87 us (2%)
  waiting for transfers between devices  1.85 us (2%)
    ppermute x6, starting transfers between devices, extended(): after = lax.ppermute(initial, axis, down)  9.53 us
    ppermute x6, starting transfers between devices, extended(): before = lax.ppermute(last, axis, up)  7.3 us
    dot_general x2, matrix products, cell_energy(): jnp.dot(latent, w_mix, preferred_element_type=jnp.float32)  4.99 us
    reduce_sum x2, other arithmetic, cell_energy(): project = jnp.repeat(environment, neigh_count, axis=0) * harm[:, None, :]  4.02 us
    gather x6, local copies, waits for them, and re-layouts, pack_side(): feat_rows[ghost_sel]  3.98 us
    gather x6, local copies, waits for them, and re-layouts, pack_side(): places16[:, ghost_sel]  3.68 us
    unnamed x67, local copies, waits for them, and re-layouts  3.63 us
    dot_general x2, matrix products, cell_energy(): before = before + jnp.dot(basis, w_radial, precision=lax.Precision.HIGHEST)  3.59 us
  transfers between devices with their start and end apart: 12, of which 1 were waited for; matrix products, arithmetic and copies ran while one was open for 26% of the time, Pallas kernels for 0%

commit v1 on v0

v1 whole, which is shorter than its diff:
```python
import functools
import math

import jax
import jax.numpy as jnp
from jax import lax
from jax.experimental import pallas as pl
from jax.experimental.pallas import tpu as pltpu
from jax.sharding import PartitionSpec as P

cell_edge = 2.0
basis_width = 0.5
f32 = jnp.float32
bf16 = jnp.bfloat16
NT = (((1,), (1,)), ((), ()))
TN = (((0,), (0,)), ((), ()))
NN = (((1,), (0,)), ((), ()))


def dot(a, b, dims=NN):
    return lax.dot_general(a, b, dims, preferred_element_type=f32)


def slots_of(axes):
    slots = []
    for a, (_, size) in enumerate(axes):
        slots += [(a, (0, 1))] if size == 2 else [(a, (0,)), (a, (1,))]
    return slots


def sigmoid(x):
    return 0.5 * jnp.tanh(0.5 * x) + 0.5


def split(x):
    high = x.astype(bf16).astype(f32)
    return high, x - high


def kernel(
    axes,
    pos_ref,
    feat_ref,
    gl_ref,
    ml_ref,
    nb_ref,
    w_rad_ref,
    w_env_ref,
    w_scal_ref,
    w_out_ref,
    w_self_hbm,
    w_pair_hbm,
    w_mix_hbm,
    w_upd_hbm,
    force_ref,
    energy_ref,
    mpos_ref,
    mfeat_ref,
    w_self_ref,
    w_pair_ref,
    w_mix_ref,
    w_upd_ref,
    small_tx,
    small_rx,
    feats,
    grad_tx,
    grad_rx,
    w_sem,
    small_send,
    small_recv,
    feat_send,
    feat_recv,
    grad_send,
    grad_recv,
):
    atoms = pos_ref.shape[1]
    ghosts = gl_ref.shape[2]
    moves = ml_ref.shape[2]
    neigh = nb_ref.shape[0]
    edges = neigh * atoms
    ext = atoms + 6 * ghosts
    radial = w_rad_ref.shape[0]
    channels = w_env_ref.shape[1]
    slots = slots_of(axes)
    rows = atoms * (len(slots) + 1)
    slot_of = {(a, side): s for s, (a, sides) in enumerate(slots) for side in sides}

    def device(a, step):
        name, size = axes[a]
        return {name: lax.rem(lax.axis_index(name) + (step % size), size)}

    weights = []
    for q, (src, dst) in enumerate(
        (
            (w_pair_hbm, w_pair_ref),
            (w_self_hbm, w_self_ref),
            (w_mix_hbm, w_mix_ref),
            (w_upd_hbm, w_upd_ref),
        )
    ):
        copy = pltpu.make_async_copy(src, dst, w_sem.at[q])
        copy.start()
        weights.append(copy)

    barrier = pltpu.get_barrier_semaphore()
    for a, sides in slots:
        step = 1 if sides[0] == 0 else -1
        pl.semaphore_signal(
            barrier, inc=1, device_id=device(a, step), device_id_type=pl.DeviceIdType.MESH
        )

    small_tx[...] = jnp.zeros_like(small_tx)
    small_tx[0:3, 0:atoms] = pos_ref[...].astype(f32)
    for a in range(3):
        small_tx[8 + 2 * a : 10 + 2 * a, 0:ghosts] = gl_ref[a].astype(f32)
        small_tx[16 + 2 * a : 18 + 2 * a, 0:moves] = ml_ref[a].astype(f32)

    pl.semaphore_wait(barrier, len(slots))

    small_copies, feat_copies = [], []
    for s, (a, sides) in enumerate(slots):
        copy = pltpu.make_async_remote_copy(
            src_ref=small_tx,
            dst_ref=small_rx.at[s],
            send_sem=small_send.at[s],
            recv_sem=small_recv.at[s],
            device_id=device(a, 1 if sides[0] == 0 else -1),
            device_id_type=pl.DeviceIdType.MESH,
        )
        copy.start()
        small_copies.append(copy)
    for s, (a, sides) in enumerate(slots):
        copy = pltpu.make_async_remote_copy(
            src_ref=feat_ref,
            dst_ref=feats.at[pl.ds(atoms * (s + 1), atoms)],
            send_sem=feat_send.at[s],
            recv_sem=feat_recv.at[s],
            device_id=device(a, 1 if sides[0] == 0 else -1),
            device_id_type=pl.DeviceIdType.MESH,
        )
        copy.start()
        feat_copies.append(copy)

    own = feat_ref[...]
    feats[0:atoms, :] = own

    nb = nb_ref[...]
    nb_row = jnp.concatenate([nb[k : k + 1, :] for k in range(neigh)], axis=1)
    hot_ext = jnp.where(
        lax.broadcasted_iota(jnp.int32, (ext, edges), 0) == nb_row, 1.0, 0.0
    ).astype(bf16)
    places = small_tx[0:3, 0:atoms]

    def tile_atoms(x):
        return jnp.concatenate([x] * neigh, axis=1)

    centre = tile_atoms(places)
    shifts = []
    for a in range(3):
        start = atoms + 2 * a * ghosts
        lower = (nb_row >= start) & (nb_row < start + ghosts)
        upper = (nb_row >= start + ghosts) & (nb_row < start + 2 * ghosts)
        shifts.append(jnp.where(lower, -cell_edge, jnp.where(upper, cell_edge, 0.0)))
    w_env_t = jnp.transpose(w_env_ref[...].astype(f32)).astype(bf16)
    out_id = lax.broadcasted_iota(jnp.int32, (3 * channels, 3 * channels), 0)
    in_id = lax.broadcasted_iota(jnp.int32, (3 * channels, 3 * channels), 1)
    permute = jnp.where(
        in_id == (out_id % channels) * 3 + out_id // channels, 1.0, 0.0
    ).astype(bf16)
    w_scal = dot(permute, w_scal_ref[...].astype(bf16)).astype(bf16)
    w_rad_high, w_rad_low = split(w_rad_ref[...])
    w_out = w_out_ref[...]

    weights[1].wait()
    self_proj = dot(own, w_self_ref[...]).astype(bf16).astype(f32)

    for copy in small_copies:
        copy.wait_recv()
    pieces = [lax.broadcasted_iota(jnp.int32, (1, atoms), 1)]
    for q in range(6):
        a, side = q // 2, q % 2
        s = slot_of[(a, side)]
        row = 8 + 2 * a + 1 - side
        listed = small_rx[s, row : row + 1, 0:ghosts].astype(jnp.int32)
        pieces.append(listed + atoms * (s + 1))
    owner_row = jnp.concatenate(pieces, axis=1)
    hot_owner = jnp.where(
        lax.broadcasted_iota(jnp.int32, (rows, ext), 0) == owner_row, 1.0, 0.0
    ).astype(bf16)
    hot_t_wide = dot(hot_owner, hot_ext)
    hot_t = hot_t_wide.astype(bf16)
    hot = jnp.transpose(hot_t_wide).astype(bf16)
    places_all = jnp.concatenate(
        [small_tx[0:8, 0:atoms]] + [small_rx[s, 0:8, 0:atoms] for s in range(len(slots))], axis=1
    ).astype(bf16)
    partner = dot(places_all, hot_t)
    offset = [partner[a : a + 1, :] + shifts[a] - centre[a : a + 1, :] for a in range(3)]
    dist = jnp.sqrt(offset[0] * offset[0] + offset[1] * offset[1] + offset[2] * offset[2] + 0.25)
    inverse = 1.0 / dist
    ux, uy, uz = [o * inverse for o in offset]
    root3 = math.sqrt(3.0)
    root15 = math.sqrt(15.0)
    root5 = math.sqrt(5.0)
    harm = [
        None,
        root3 * ux,
        root3 * uy,
        root3 * uz,
        root15 * ux * uy,
        root15 * uy * uz,
        0.5 * root5 * (3.0 * uz * uz - 1.0),
        root15 * ux * uz,
        0.5 * root15 * (ux * ux - uy * uy),
    ]
    degree = [0, 1, 1, 1, 2, 2, 2, 2, 2]
    centres = basis_width * lax.broadcasted_iota(jnp.int32, (radial, edges), 0).astype(f32)
    away = dist - centres
    basis = jnp.exp(-jnp.square(away * (1.0 / basis_width)))
    basis_high, basis_low = split(basis)
    basis_cat = jnp.concatenate([basis_high, basis_low, basis_high], axis=0).astype(bf16)
    w_rad_cat = jnp.concatenate([w_rad_high, w_rad_high, w_rad_low], axis=0).astype(bf16)
    before = dot(basis_cat, w_rad_cat, TN) + jnp.concatenate([self_proj] * neigh, axis=0)

    weights[0].wait()
    for copy in feat_copies:
        copy.wait_recv()
    pair = dot(feats[...], w_pair_ref[...]).astype(bf16)
    before = before + dot(hot, pair)

    def silu_pair(x):
        gate = sigmoid(x)
        value = x * gate
        return value, gate + value * (1.0 - gate)

    latent, slope_a = silu_pair(before)
    weights[2].wait()
    mixed, slope_z = silu_pair(dot(latent.astype(bf16), w_mix_ref[...]))
    mixed = mixed.astype(bf16)
    env_w = dot(w_env_t, mixed, NT)

    def over_neighbours(x):
        total = x[:, 0:128]
        for q in range(1, edges // 128):
            total = total + x[:, 128 * q : 128 * (q + 1)]
        total = total + pltpu.roll(total, 64, 1)
        return jnp.concatenate([total] * (edges // 128), axis=1)

    scale = 1.0 / math.sqrt(neigh)

    def times(x, m):
        return x if harm[m] is None else x * harm[m]

    environment = [over_neighbours(times(env_w, m)) * scale for m in range(9)]
    invariants = [None, None, None]
    for m in range(9):
        term = times(environment[m], m)
        level = degree[m]
        invariants[level] = term if invariants[level] is None else invariants[level] + term
    invariants = jnp.concatenate(invariants, axis=0).astype(bf16)
    weights[3].wait()
    update, slope_y = silu_pair(dot(mixed, w_upd_ref[...]) + dot(invariants, w_scal, TN))
    total = update[0:atoms, :]
    for k in range(1, neigh):
        total = total + update[atoms * k : atoms * (k + 1), :]
    energy_ref[...] = lax.dot_general(
        w_out, total, NT, precision=lax.Precision.HIGHEST, preferred_element_type=f32
    )

    d_y = (slope_y * w_out).astype(bf16)
    d_inv = dot(w_scal, d_y, NT)
    d_harm = [None] * 9
    d_env_w = None
    for m in range(9):
        d_level = d_inv[channels * degree[m] : channels * (degree[m] + 1), :]
        d_environment = over_neighbours(times(d_level, m)) * scale
        back = times(d_environment, m)
        d_env_w = back if d_env_w is None else d_env_w + back
        if m:
            d_harm[m] = jnp.sum(
                d_level * environment[m] + d_environment * env_w, axis=0, keepdims=True
            )
    d_mixed = dot(d_y, w_upd_ref[...], NT) + dot(d_env_w.astype(bf16), w_env_t, TN)
    d_z = (slope_z * d_mixed).astype(bf16)
    d_before = (slope_a * dot(d_z, w_mix_ref[...], NT)).astype(bf16)
    w_rad_two = jnp.concatenate([w_rad_high, w_rad_low], axis=0).astype(bf16)
    d_basis = dot(w_rad_two, d_before, NT)
    d_basis = d_basis[0:radial, :] + d_basis[radial : 2 * radial, :]
    d_dist = jnp.sum(
        d_basis * basis * away * (-2.0 / basis_width**2), axis=0, keepdims=True
    )
    d_ux = root3 * d_harm[1] + root15 * (uy * d_harm[4] + uz * d_harm[7] + ux * d_harm[8])
    d_uy = root3 * d_harm[2] + root15 * (ux * d_harm[4] + uz * d_harm[5] - uy * d_harm[8])
    d_uz = (
        root3 * d_harm[3]
        + root15 * (uy * d_harm[5] + ux * d_harm[7])
        + (3.0 * root5) * uz * d_harm[6]
    )
    along = d_dist - (d_ux * ux + d_uy * uy + d_uz * uz) * inverse
    d_offset = jnp.concatenate(
        [
            d_ux * inverse + ux * along,
            d_uy * inverse + uy * along,
            d_uz * inverse + uz * along,
            jnp.zeros((5, edges), f32),
        ],
        axis=0,
    )
    d_high, d_low = split(d_offset)
    scattered = dot(jnp.concatenate([d_high, d_low], axis=0).astype(bf16), hot_t, NT)
    scattered = scattered[0:8, :] + scattered[8:16, :]
    for s in range(len(slots)):
        grad_tx[s, :, 0:atoms] = scattered[:, atoms * (s + 1) : atoms * (s + 2)]
    grad_copies = []
    for s, (a, sides) in enumerate(slots):
        copy = pltpu.make_async_remote_copy(
            src_ref=grad_tx.at[s],
            dst_ref=grad_rx.at[s],
            send_sem=grad_send.at[s],
            recv_sem=grad_recv.at[s],
            device_id=device(a, -1 if sides[0] == 0 else 1),
            device_id_type=pl.DeviceIdType.MESH,
        )
        copy.start()
        grad_copies.append(copy)
    gradient = scattered[:, 0:atoms] - over_neighbours(d_offset)[:, 0:atoms]

    slot_row = jnp.concatenate(
        [small_tx[16 + q : 17 + q, 0:moves] for q in range(6)], axis=1
    ).astype(jnp.int32)
    from_row = jnp.concatenate(
        [
            small_rx[slot_of[(q // 2, q % 2)], 16 + (q ^ 1) : 17 + (q ^ 1), 0:moves].astype(
                jnp.int32
            )
            + atoms * (slot_of[(q // 2, q % 2)] + 1)
            for q in range(6)
        ],
        axis=1,
    )
    slot_hot = jnp.where(
        lax.broadcasted_iota(jnp.int32, (atoms, 6 * moves), 0) == slot_row, 1.0, 0.0
    )
    from_hot = jnp.where(
        lax.broadcasted_iota(jnp.int32, (rows, 6 * moves), 0) == from_row, 1.0, 0.0
    ).astype(bf16)
    keeps = 1.0 - jnp.sum(slot_hot, axis=1, keepdims=True)
    same = lax.broadcasted_iota(jnp.int32, (atoms, rows), 0) == lax.broadcasted_iota(
        jnp.int32, (atoms, rows), 1
    )
    slot_hot = slot_hot.astype(bf16)
    source = (dot(slot_hot, from_hot, NT) + jnp.where(same, keeps, 0.0)).astype(bf16)
    mfeat_ref[...] = dot(source, feats[...]).astype(bf16)
    entry = lax.broadcasted_iota(jnp.int32, (8, 6 * moves), 1) // moves
    along_row = lax.broadcasted_iota(jnp.int32, (8, 6 * moves), 0)
    move_shift = jnp.where(
        entry == 2 * along_row, -cell_edge, jnp.where(entry == 2 * along_row + 1, cell_edge, 0.0)
    ).astype(bf16)
    moved = dot(places_all, source, NT) + dot(move_shift, slot_hot, NT)
    mpos_ref[...] = moved[0:3, :].astype(bf16)

    for s, copy in enumerate(grad_copies):
        copy.wait_recv()
        gradient = gradient + grad_rx[s, :, 0:atoms]
    force_ref[...] = -gradient[0:3, :]
    for copy in small_copies + feat_copies + grad_copies:
        copy.wait_send()


def shards(axes, *args):
    (
        positions,
        features,
        ghost_lists,
        move_lists,
        neighbours,
        w_self,
        w_pair,
        w_radial,
        w_mix,
        w_env,
        w_scal,
        w_upd,
        w_out,
    ) = args
    atoms = positions.shape[-1]
    width = features.shape[-1]
    count = len(slots_of(axes))
    in_vmem = pl.BlockSpec(memory_space=pltpu.VMEM)
    anywhere = pl.BlockSpec(memory_space=pl.ANY)
    semaphores = pltpu.SemaphoreType.DMA((count,))
    forces, energy, moved_positions, moved_features = pl.pallas_call(
        functools.partial(kernel, axes),
        out_shape=(
            jax.ShapeDtypeStruct((3, atoms), f32),
            jax.ShapeDtypeStruct((1, atoms), f32),
            jax.ShapeDtypeStruct((3, atoms), bf16),
            jax.ShapeDtypeStruct((atoms, width), bf16),
        ),
        in_specs=[in_vmem] * 9 + [anywhere] * 4,
        out_specs=(in_vmem,) * 4,
        scratch_shapes=[pltpu.VMEM((width, width), bf16)] * 4
        + [
            pltpu.VMEM((24, 128), f32),
            pltpu.VMEM((count, 24, 128), f32),
            pltpu.VMEM((atoms * (count + 1), width), bf16),
            pltpu.VMEM((count, 8, 128), f32),
            pltpu.VMEM((count, 8, 128), f32),
            pltpu.SemaphoreType.DMA((4,)),
        ]
        + [semaphores] * 6,
        compiler_params=pltpu.CompilerParams(
            collective_id=0, has_side_effects=True, vmem_limit_bytes=40 * 1024 * 1024
        ),
    )(
        positions.reshape(positions.shape[3:]),
        features.reshape(features.shape[3:]),
        ghost_lists.reshape(ghost_lists.shape[3:]),
        move_lists.reshape(move_lists.shape[3:]),
        neighbours.reshape(neighbours.shape[3:]),
        w_radial,
        w_env,
        w_scal,
        w_out.reshape(1, -1),
        w_self,
        w_pair,
        w_mix,
        w_upd,
    )
    return (
        forces.reshape(positions.shape),
        energy.reshape(1, 1, 1, atoms),
        moved_positions.reshape(positions.shape),
        moved_features.reshape(features.shape),
    )


def solution(mesh):
    axes = tuple((name, mesh.shape[name]) for name in ("gx", "gy", "gz"))
    cell = P("gx", "gy", "gz", None, None)
    lists = P("gx", "gy", "gz", None, None, None)
    return jax.shard_map(
        functools.partial(shards, axes),
        mesh=mesh,
        in_specs=(cell, cell, lists, lists, cell) + (P(),) * 8,
        out_specs=(cell, P("gx", "gy", "gz", None), cell, cell),
        check_vma=False,
    )
```

time: 86.3 us -> 28.5 us (0.33)
  other arithmetic: 21.6 us -> 0 us
  local copies, waits for them, and re-layouts: 29.6 us -> 8.31 us
  Pallas kernels: 0 us -> 19.1 us
  starting transfers between devices: 16.8 us -> 0 us
  matrix products: 13.8 us -> 0 us
  waiting for transfers between devices: 1.85 us -> 0 us
  between operations: 1.87 us -> 0.77 us
    pallas_call x0 -> x1, Pallas kernels: none -> 19.1 us  [shards(): pl.pallas_call(functools.partial(kernel, axes), out_shape=(jax.ShapeDtype...]
    gather x27 -> x0, local copies, waits for them, and re-layouts: 17.5 us -> none  [the longest x6 3.98 us: pack_side(): feat_rows[ghost_sel]]
    ppermute x12 -> x0, starting transfers between devices: 16.8 us -> none  [the longest x6 9.53 us: extended(): after = lax.ppermute(initial, axis, down)]
    dot_general x12 -> x0, matrix products: 13.8 us -> none  [the longest x2 4.99 us: cell_energy(): jnp.dot(latent, w_mix, preferred_element_type=jnp.float32)]
    scatter-add x7 -> x0, other arithmetic: 8.72 us -> none  [the longest x1 3.35 us: cell_energy(): offset = ext_pos[:, flat_index] - centre]
    reduce_sum x10 -> x0, other arithmetic: 5.39 us -> none  [the longest x2 4.02 us: cell_energy(): project = jnp.repeat(environment, neigh_count, axis=0) * harm[:, None, :]]
    scatter x6 -> x0, local copies, waits for them, and re-layouts: 5.13 us -> none  [the longest x3 2.58 us: shards(): moved_feat.at[move_idx[direction, 1]].set(arrived[3, ghost_count:, :width])]
    scatter x6 -> x0, other arithmetic: 4.86 us -> none  [the longest x3 2.43 us: shards(): moved_pos.at[:, move_idx[direction, 0]]]
  transfers between devices with their start and end apart: 12 -> 0, of which waited for: 1 -> 0; matrix products, arithmetic and copies ran while one was open for 26% -> 0% of each run, Pallas kernels for 0% -> 0%
where the time goes in v1:
time: 28.5 us; the launch traced here: 28.2 us
  Pallas kernels  19.1 us (67%)
  local copies, waits for them, and re-layouts  8.31 us (29%)
  between operations  0.77 us (3%)
    pallas_call x1, Pallas kernels, shards(): pl.pallas_call(functools.partial(kernel, axes), out_shape=(jax.ShapeDtype...  19.1 us
    unnamed x29, local copies, waits for them, and re-layouts  8.31 us

profile of v1, /device:TPU:0, one launch (start us, length us, event | category | flops | bytes accessed | tf_op | source)
XLA Modules:
  0.0 28.2 jit_solution(6873992943354877332)
XLA Ops:
  0.6 0.0 copy-start.5
  0.6 0.0 copy-start.6
  0.7 0.0 copy-start.7
  0.7 0.0 copy-start.8
  0.7 0.0 copy-start.9
  0.7 0.0 copy-start.10
  0.7 0.0 copy-start.11
  0.7 0.9 %copy.17.w_env_ref = bf16[512,32]{1,0:T(8,128)(2,1)S(1)} copy(bf16[512,32]{0,1:T(8,128)(2,1)} %param.22) | data formatting | bytes 65536 | tf_op args[9]
  1.6 0.0 copy-done.5
  1.6 0.0 copy-done.6
  1.7 0.0 copy-done.7
  1.7 0.0 copy-done.8
  1.7 0.0 copy-done.9
  1.7 0.0 copy-done.10
  1.7 0.0 copy-done.11
  1.7 0.0 copy-start
  1.7 1.0 %copy-done = bf16[512,512]{1,0:T(8,128)(2,1)S(1)} copy-done((bf16[512,512]{1,0:T(8,128)(2,1)S(1)}, bf16[512,512]{1,0:T(8,128)(2,1)}, u32[]{:S(2)}) %copy-start) | copy-done | bytes 524312
  2.8 0.0 copy-start.1
  2.8 1.0 %copy-done.1 = bf16[512,512]{1,0:T(8,128)(2,1)S(1)} copy-done((bf16[512,512]{1,0:T(8,128)(2,1)S(1)}, bf16[512,512]{1,0:T(8,128)(2,1)}, u32[]{:S(2)}) %copy-start.1) | copy-done | bytes 524312
  3.8 0.0 copy-start.2
  3.8 1.0 %copy-done.2 = bf16[512,512]{1,0:T(8,128)(2,1)S(1)} copy-done((bf16[512,512]{1,0:T(8,128)(2,1)S(1)}, bf16[512,512]{1,0:T(8,128)(2,1)}, u32[]{:S(2)}) %copy-start.2) | copy-done | bytes 524312
  4.8 0.0 copy-start.3
  4.8 1.0 %copy-done.3 = bf16[512,512]{1,0:T(8,128)(2,1)S(1)} copy-done((bf16[512,512]{1,0:T(8,128)(2,1)S(1)}, bf16[512,512]{1,0:T(8,128)(2,1)}, u32[]{:S(2)}) %copy-start.3) | copy-done | bytes 524312
  5.9 0.0 copy-start.4
  5.9 0.9 %copy-done.4 = f32[96,512]{1,0:T(8,128)S(1)} copy-done((f32[96,512]{1,0:T(8,128)S(1)}, f32[96,512]{1,0:T(8,128)}, u32[]{:S(2)}) %copy-start.4) | copy-done | bytes 196632
  6.8 19.1 %shard_map.156 = (f32[3,64]{1,0:T(4,128)S(1)}, f32[1,64]{1,0:T(1,128)S(1)}, bf16[3,64]{1,0:T(4,128)(2,1)S(1)}, bf16[64,512]{1,0:T(8,128)(2,1)S(1)}) custom-call(bf16[3,64]{1,0:T(4,128)(2,1)S(1)} %bitcast.17, bf16[64,512]{1,0:T(8,128)(2,1)S(1)} %bitcast.10, s32[3,2,48]{2,1,0:T(2,128)S(1)} %bitcast.13, s32[3,2,4]{2,1,0:T(2,128)S(1)} %bitcast.14, ...), custom_call_target="tpu_custom_call" | custom-call | tf_op jit(solution)/shard_map/pallas_call | solution.py:391
  25.9 0.6 %copy.18 = f32[1,1,1,3,64]{4,2,3,1,0:T(1,128)} copy(f32[1,1,1,3,64]{4,3,2,1,0:T(4,128)S(1)} %bitcast.16) | data formatting | bytes 1536
  26.5 0.5 %copy.22 = f32[1,1,1,64]{3,2,1,0:T(1,128)} copy(f32[1,1,1,64]{3,2,1,0:T(1,128)S(1)} %bitcast.19) | data formatting | bytes 512
  27.0 0.6 %copy.23 = bf16[1,1,1,3,64]{4,3,2,1,0:T(4,128)(2,1)} copy(bf16[1,1,1,3,64]{4,3,2,1,0:T(4,128)(2,1)S(1)} %bitcast.18) | data formatting | bytes 768
  27.5 0.6 %copy.24 = bf16[1,1,1,64,512]{4,3,2,1,0:T(8,128)(2,1)} copy(bf16[1,1,1,64,512]{4,3,2,1,0:T(8,128)(2,1)S(1)} %bitcast.11) | data formatting | bytes 131072
Async XLA Ops:
  0.6 1.0 %copy-start.5 = (bf16[1,1,1,64,512]{4,3,2,1,0:T(8,128)(2,1)S(1)}, bf16[1,1,1,64,512]{4,3,2,1,0:T(8,128)(2,1)}, u32[]{:S(2)}) copy-start(bf16[1,1,1,64,512]{4,3,2,1,0:T(8,128)(2,1)} %param.14) | copy-start | bytes 196612
  0.6 1.0 %copy-start.6 = (f32[8,512]{1,0:T(8,128)S(1)}, f32[8,512]{1,0:T(8,128)}, u32[]{:S(2)}) copy-start(f32[8,512]{1,0:T(8,128)} %w_rad_ref.1) | copy-start | bytes 49156
  0.7 1.0 %copy-start.7 = (s32[1,1,1,8,64]{4,3,2,1,0:T(8,128)S(1)}, s32[1,1,1,8,64]{4,3,2,1,0:T(8,128)}, u32[]{:S(2)}) copy-start(s32[1,1,1,8,64]{4,3,2,1,0:T(8,128)} %param.17) | copy-start | bytes 6148
  0.7 1.0 %copy-start.8 = (s32[1,1,1,3,2,48]{5,4,3,2,1,0:T(2,128)S(1)}, s32[1,1,1,3,2,48]{5,4,3,2,1,0:T(2,128)}, u32[]{:S(2)}) copy-start(s32[1,1,1,3,2,48]{5,4,3,2,1,0:T(2,128)} %param.15) | copy-start | bytes 3460
  0.7 1.0 %copy-start.9 = (s32[1,1,1,3,2,4]{5,4,3,2,1,0:T(2,128)S(1)}, s32[1,1,1,3,2,4]{5,4,3,2,1,0:T(2,128)}, u32[]{:S(2)}) copy-start(s32[1,1,1,3,2,4]{5,4,3,2,1,0:T(2,128)} %param.16) | copy-start | bytes 292
  0.7 1.0 %copy-start.10 = (f32[512]{0:T(512)S(1)}, f32[512]{0:T(512)}, u32[]{:S(2)}) copy-start(f32[512]{0:T(512)} %param.25) | copy-start | bytes 6148
  0.7 1.0 %copy-start.11 = (bf16[1,1,1,3,64]{4,3,2,1,0:T(4,128)(2,1)S(1)}, bf16[1,1,1,3,64]{4,3,2,1,0:T(4,128)(2,1)}, u32[]{:S(2)}) copy-start(bf16[1,1,1,3,64]{4,3,2,1,0:T(4,128)(2,1)} %param.13) | copy-start | bytes 1156
  1.7 1.0 %copy-start = (bf16[512,512]{1,0:T(8,128)(2,1)S(1)}, bf16[512,512]{1,0:T(8,128)(2,1)}, u32[]{:S(2)}) copy-start(bf16[512,512]{1,0:T(8,128)(2,1)} %w_self_hbm.1) | copy-start | bytes 1572868
  2.8 1.0 %copy-start.1 = (bf16[512,512]{1,0:T(8,128)(2,1)S(1)}, bf16[512,512]{1,0:T(8,128)(2,1)}, u32[]{:S(2)}) copy-start(bf16[512,512]{1,0:T(8,128)(2,1)} %w_pair_hbm.1) | copy-start | bytes 1572868
  3.8 1.0 %copy-start.2 = (bf16[512,512]{1,0:T(8,128)(2,1)S(1)}, bf16[512,512]{1,0:T(8,128)(2,1)}, u32[]{:S(2)}) copy-start(bf16[512,512]{1,0:T(8,128)(2,1)} %w_mix_hbm.1) | copy-start | bytes 1572868
  4.8 1.0 %copy-start.3 = (bf16[512,512]{1,0:T(8,128)(2,1)S(1)}, bf16[512,512]{1,0:T(8,128)(2,1)}, u32[]{:S(2)}) copy-start(bf16[512,512]{1,0:T(8,128)(2,1)} %w_upd_hbm.1) | copy-start | bytes 1572868
  5.9 0.9 %copy-start.4 = (f32[96,512]{1,0:T(8,128)S(1)}, f32[96,512]{1,0:T(8,128)}, u32[]{:S(2)}) copy-start(f32[96,512]{1,0:T(8,128)} %w_scal_ref.1) | copy-start | bytes 589828

commit v2 on v1

--- a/solution.py
+++ b/solution.py
@@ -8,6 +8,7 @@
 from jax.experimental.pallas import tpu as pltpu
 from jax.sharding import PartitionSpec as P
 
+VMEM_BYTES = 63 * 1024 * 1024 + 768 * 1024
 cell_edge = 2.0
 basis_width = 0.5
 f32 = jnp.float32
@@ -39,8 +40,24 @@
 
 def kernel(
     axes,
+    pos_hbm,
+    feat_hbm,
+    gl_hbm,
+    ml_hbm,
+    nb_hbm,
+    w_rad_hbm,
+    w_env_hbm,
+    w_scal_hbm,
+    w_out_hbm,
+    w_self_hbm,
+    w_pair_hbm,
+    w_mix_hbm,
+    w_upd_hbm,
+    force_hbm,
+    energy_hbm,
+    mpos_hbm,
+    mfeat_hbm,
     pos_ref,
-    feat_ref,
     gl_ref,
     ml_ref,
     nb_ref,
@@ -48,14 +65,6 @@
     w_env_ref,
     w_scal_ref,
     w_out_ref,
-    w_self_hbm,
-    w_pair_hbm,
-    w_mix_hbm,
-    w_upd_hbm,
-    force_ref,
-    energy_ref,
-    mpos_ref,
-    mfeat_ref,
     w_self_ref,
     w_pair_ref,
     w_mix_ref,
@@ -65,7 +74,12 @@
     feats,
     grad_tx,
     grad_rx,
-    w_sem,
+    force_ref,
+    energy_ref,
+    mpos_ref,
+    mfeat_ref,
+    load_sem,
+    store_sem,
     small_send,
     small_recv,
     feat_send,
@@ -80,7 +94,7 @@
     edges = neigh * atoms
     ext = atoms + 6 * ghosts
     radial = w_rad_ref.shape[0]
-    channels = w_env_ref.shape[1]
+    channels = w_env_ref.shape[0]
     slots = slots_of(axes)
     rows = atoms * (len(slots) + 1)
     slot_of = {(a, side): s for s, (a, sides) in enumerate(slots) for side in sides}
@@ -88,19 +102,6 @@
     def device(a, step):
         name, size = axes[a]
         return {name: lax.rem(lax.axis_index(name) + (step % size), size)}
-
-    weights = []
-    for q, (src, dst) in enumerate(
-        (
-            (w_pair_hbm, w_pair_ref),
-            (w_self_hbm, w_self_ref),
-            (w_mix_hbm, w_mix_ref),
-            (w_upd_hbm, w_upd_ref),
-        )
-    ):
-        copy = pltpu.make_async_copy(src, dst, w_sem.at[q])
-        copy.start()
-        weights.append(copy)
 
     barrier = pltpu.get_barrier_semaphore()
     for a, sides in slots:
@@ -109,7 +110,30 @@
             barrier, inc=1, device_id=device(a, step), device_id_type=pl.DeviceIdType.MESH
         )
 
+    loads = {}
+    for q, (name, src, dst) in enumerate(
+        (
+            ("pos", pos_hbm, pos_ref),
+            ("gl", gl_hbm, gl_ref),
+            ("ml", ml_hbm, ml_ref),
+            ("nb", nb_hbm, nb_ref),
+            ("feat", feat_hbm, feats.at[pl.ds(0, atoms)]),
+            ("self", w_self_hbm, w_self_ref),
+            ("scal", w_scal_hbm, w_scal_ref),
+            ("rad", w_rad_hbm, w_rad_ref),
+            ("env", w_env_hbm, w_env_ref),
+            ("out", w_out_hbm, w_out_ref),
+            ("pair", w_pair_hbm, w_pair_ref),
+            ("mix", w_mix_hbm, w_mix_ref),
+            ("upd", w_upd_hbm, w_upd_ref),
+        )
+    ):
+        loads[name] = pltpu.make_async_copy(src, dst, load_sem.at[q])
+        loads[name].start()
+
     small_tx[...] = jnp.zeros_like(small_tx)
+    for name in ("pos", "gl", "ml"):
+        loads[name].wait()
     small_tx[0:3, 0:atoms] = pos_ref[...].astype(f32)
     for a in range(3):
         small_tx[8 + 2 * a : 10 + 2 * a, 0:ghosts] = gl_ref[a].astype(f32)
@@ -131,7 +155,7 @@
         small_copies.append(copy)
     for s, (a, sides) in enumerate(slots):
         copy = pltpu.make_async_remote_copy(
-            src_ref=feat_ref,
+            src_ref=feat_hbm,
             dst_ref=feats.at[pl.ds(atoms * (s + 1), atoms)],
             send_sem=feat_send.at[s],
             recv_sem=feat_recv.at[s],
@@ -141,9 +165,7 @@
         copy.start()
         feat_copies.append(copy)
 
-    own = feat_ref[...]
-    feats[0:atoms, :] = own
-
+    loads["nb"].wait()
     nb = nb_ref[...]
     nb_row = jnp.concatenate([nb[k : k + 1, :] for k in range(neigh)], axis=1)
     hot_ext = jnp.where(
@@ -161,7 +183,9 @@
         lower = (nb_row >= start) & (nb_row < start + ghosts)
         upper = (nb_row >= start + ghosts) & (nb_row < start + 2 * ghosts)
         shifts.append(jnp.where(lower, -cell_edge, jnp.where(upper, cell_edge, 0.0)))
-    w_env_t = jnp.transpose(w_env_ref[...].astype(f32)).astype(bf16)
+    for name in ("scal", "rad", "env", "out", "feat", "self"):
+        loads[name].wait()
+    w_env_t = w_env_ref[...]
     out_id = lax.broadcasted_iota(jnp.int32, (3 * channels, 3 * channels), 0)
     in_id = lax.broadcasted_iota(jnp.int32, (3 * channels, 3 * channels), 1)
     permute = jnp.where(
@@ -171,8 +195,7 @@
     w_rad_high, w_rad_low = split(w_rad_ref[...])
     w_out = w_out_ref[...]
 
-    weights[1].wait()
-    self_proj = dot(own, w_self_ref[...]).astype(bf16).astype(f32)
+    self_proj = dot(feats[0:atoms, :], w_self_ref[...]).astype(bf16).astype(f32)
 
     for copy in small_copies:
         copy.wait_recv()
@@ -221,7 +244,7 @@
     w_rad_cat = jnp.concatenate([w_rad_high, w_rad_high, w_rad_low], axis=0).astype(bf16)
     before = dot(basis_cat, w_rad_cat, TN) + jnp.concatenate([self_proj] * neigh, axis=0)
 
-    weights[0].wait()
+    loads["pair"].wait()
     for copy in feat_copies:
         copy.wait_recv()
     pair = dot(feats[...], w_pair_ref[...]).astype(bf16)
@@ -233,7 +256,7 @@
         return value, gate + value * (1.0 - gate)
 
     latent, slope_a = silu_pair(before)
-    weights[2].wait()
+    loads["mix"].wait()
     mixed, slope_z = silu_pair(dot(latent.astype(bf16), w_mix_ref[...]))
     mixed = mixed.astype(bf16)
     env_w = dot(w_env_t, mixed, NT)
@@ -257,7 +280,7 @@
         level = degree[m]
         invariants[level] = term if invariants[level] is None else invariants[level] + term
     invariants = jnp.concatenate(invariants, axis=0).astype(bf16)
-    weights[3].wait()
+    loads["upd"].wait()
     update, slope_y = silu_pair(dot(mixed, w_upd_ref[...]) + dot(invariants, w_scal, TN))
     total = update[0:atoms, :]
     for k in range(1, neigh):
@@ -265,6 +288,9 @@
     energy_ref[...] = lax.dot_general(
         w_out, total, NT, precision=lax.Precision.HIGHEST, preferred_element_type=f32
     )
+
+    energy_copy = pltpu.make_async_copy(energy_ref, energy_hbm, store_sem.at[0])
+    energy_copy.start()
 
     d_y = (slope_y * w_out).astype(bf16)
     d_inv = dot(w_scal, d_y, NT)
@@ -357,13 +383,33 @@
     ).astype(bf16)
     moved = dot(places_all, source, NT) + dot(move_shift, slot_hot, NT)
     mpos_ref[...] = moved[0:3, :].astype(bf16)
+    mfeat_copy = pltpu.make_async_copy(mfeat_ref, mfeat_hbm, store_sem.at[1])
+    mfeat_copy.start()
+    mpos_copy = pltpu.make_async_copy(mpos_ref, mpos_hbm, store_sem.at[2])
+    mpos_copy.start()
 
     for s, copy in enumerate(grad_copies):
         copy.wait_recv()
         gradient = gradient + grad_rx[s, :, 0:atoms]
-    force_ref[...] = -gradient[0:3, :]
+    for a in range(3):
+        force_ref[a] = -gradient[a : a + 1, :]
+    force_copy = pltpu.make_async_copy(force_ref, force_hbm, store_sem.at[3])
+    force_copy.start()
     for copy in small_copies + feat_copies + grad_copies:
         copy.wait_send()
+    for copy in (energy_copy, mfeat_copy, mpos_copy, force_copy):
+        copy.wait()
+
+
+def finish(*refs):
+    count = len(refs) // 2
+    copies = [
+        pltpu.make_async_copy(refs[q], refs[count + q], refs[-1].at[q]) for q in range(count)
+    ]
+    for copy in copies:
+        copy.start()
+    for copy in copies:
+        copy.wait()
 
 
 def shards(axes, *args):
@@ -385,47 +431,62 @@
     atoms = positions.shape[-1]
     width = features.shape[-1]
     count = len(slots_of(axes))
-    in_vmem = pl.BlockSpec(memory_space=pltpu.VMEM)
     anywhere = pl.BlockSpec(memory_space=pl.ANY)
     semaphores = pltpu.SemaphoreType.DMA((count,))
-    forces, energy, moved_positions, moved_features = pl.pallas_call(
+    operands = (
+        positions.reshape(positions.shape[3:]),
+        features.reshape(features.shape[3:]),
+        ghost_lists.reshape(ghost_lists.shape[3:]),
+        move_lists.reshape(move_lists.shape[3:]),
+        neighbours.reshape(neighbours.shape[3:]),
+        w_radial,
+        w_env.T,
+        w_scal,
+        w_out.reshape(1, -1),
+        w_self,
+        w_pair,
+        w_mix,
+        w_upd,
+    )
+    results = (
+        jax.ShapeDtypeStruct((3, 1, atoms), f32),
+        jax.ShapeDtypeStruct((1, atoms), f32),
+        jax.ShapeDtypeStruct((3, atoms), bf16),
+        jax.ShapeDtypeStruct((atoms, width), bf16),
+    )
+    found = pl.pallas_call(
         functools.partial(kernel, axes),
-        out_shape=(
-            jax.ShapeDtypeStruct((3, atoms), f32),
-            jax.ShapeDtypeStruct((1, atoms), f32),
-            jax.ShapeDtypeStruct((3, atoms), bf16),
-            jax.ShapeDtypeStruct((atoms, width), bf16),
-        ),
-        in_specs=[in_vmem] * 9 + [anywhere] * 4,
-        out_specs=(in_vmem,) * 4,
-        scratch_shapes=[pltpu.VMEM((width, width), bf16)] * 4
+        out_shape=results,
+        in_specs=[anywhere] * len(operands),
+        out_specs=(anywhere,) * 4,
+        scratch_shapes=[
+            pltpu.VMEM(operands[q].shape, operands[q].dtype)
+            for q in (0, 2, 3, 4, 5, 6, 7, 8, 9, 10, 11, 12)
+        ]
         + [
             pltpu.VMEM((24, 128), f32),
             pltpu.VMEM((count, 24, 128), f32),
             pltpu.VMEM((atoms * (count + 1), width), bf16),
             pltpu.VMEM((count, 8, 128), f32),
             pltpu.VMEM((count, 8, 128), f32),
+        ]
+        + [pltpu.VMEM(result.shape, result.dtype) for result in results]
+        + [
+            pltpu.SemaphoreType.DMA((len(operands),)),
             pltpu.SemaphoreType.DMA((4,)),
         ]
         + [semaphores] * 6,
         compiler_params=pltpu.CompilerParams(
-            collective_id=0, has_side_effects=True, vmem_limit_bytes=40 * 1024 * 1024
+            collective_id=0, has_side_effects=True, vmem_limit_bytes=VMEM_BYTES
         ),
-    )(
-        positions.reshape(positions.shape[3:]),
-        features.reshape(features.shape[3:]),
-        ghost_lists.reshape(ghost_lists.shape[3:]),
-        move_lists.reshape(move_lists.shape[3:]),
-        neighbours.reshape(neighbours.shape[3:]),
-        w_radial,
-        w_env,
-        w_scal,
-        w_out.reshape(1, -1),
-        w_self,
-        w_pair,
-        w_mix,
-        w_upd,
-    )
+    )(*operands)
+    forces, energy, moved_positions, moved_features = pl.pallas_call(
+        finish,
+        out_shape=results,
+        in_specs=[anywhere] * 4,
+        out_specs=(anywhere,) * 4,
+        scratch_shapes=[pltpu.SemaphoreType.DMA((4,))],
+    )(*found)
     return (
         forces.reshape(positions.shape),
         energy.reshape(1, 1, 1, atoms),

time: 28.5 us -> 23.7 us (0.83)
  local copies, waits for them, and re-layouts: 8.31 us -> 0 us
  Pallas kernels: 19.1 us -> 22.9 us
    unnamed x29 -> x0, local copies, waits for them, and re-layouts: 8.31 us -> none
    pallas_call x1 -> x2, Pallas kernels: 19.1 us -> 22.9 us  [the longest x1 19.7 us: shards(): pl.pallas_call(functools.partial(kernel, axes), out_shape=results, in_spe...]
where the time goes in v2:
time: 23.7 us; the launch traced here: 23.5 us
  Pallas kernels  22.9 us (97%)
  between operations  0.64 us (3%)
    pallas_call x1, Pallas kernels, shards(): pl.pallas_call(functools.partial(kernel, axes), out_shape=results, in_spe...  19.7 us
    pallas_call x1, Pallas kernels, shards(): pl.pallas_call(finish, out_shape=results, in_specs=[anywhere] * 4, out_sp...  3.22 us

profile of v2, /device:TPU:0, one launch (start us, length us, event | category | flops | bytes accessed | tf_op | source)
XLA Modules:
  0.0 23.5 jit_solution(15065088282761681257)
XLA Ops:
  0.6 19.7 %shard_map.156 = (f32[3,1,64]{2,1,0:T(1,128)}, f32[1,64]{1,0:T(1,128)}, bf16[3,64]{1,0:T(4,128)(2,1)}, bf16[64,512]{1,0:T(8,128)(2,1)}) custom-call(bf16[3,64]{1,0:T(4,128)(2,1)} %bitcast.19, bf16[64,512]{1,0:T(8,128)(2,1)} %bitcast.13, s32[3,2,48]{2,1,0:T(2,128)} %bitcast.16, s32[3,2,4]{2,1,0:T(2,128)} %bitcast.17, s32[8,64]{1,0:T(8,128)} %bitcast.15, ...), custom_call_target="tpu_custom_call" | custom-call | tf_op jit(solution)/shard_map/pallas_call | solution.py:457
  20.3 3.2 %shard_map.157 = (f32[3,1,64]{2,1,0:T(1,128)}, f32[1,64]{1,0:T(1,128)}, bf16[3,64]{1,0:T(4,128)(2,1)}, bf16[64,512]{1,0:T(8,128)(2,1)}) custom-call(f32[3,1,64]{2,1,0:T(1,128)} %get-tuple-element.12.refs_0_, f32[1,64]{1,0:T(1,128)} %get-tuple-element.13.refs_1_, bf16[3,64]{1,0:T(4,128)(2,1)} %get-tuple-element.14.refs_2_, ...), custom_call_target="tpu_custom_call" | custom-call | tf_op jit(solution)/shard_map/pallas_call | solution.py:483

commit v3 on v2

--- a/solution.py
+++ b/solution.py
@@ -129,6 +129,7 @@
         )
     ):
         loads[name] = pltpu.make_async_copy(src, dst, load_sem.at[q])
+    for name in ("pos", "gl", "ml", "nb"):
         loads[name].start()
 
     small_tx[...] = jnp.zeros_like(small_tx)
@@ -164,6 +165,9 @@
         )
         copy.start()
         feat_copies.append(copy)
+
+    for name in list(loads)[4:]:
+        loads[name].start()
 
     loads["nb"].wait()
     nb = nb_ref[...]
@@ -402,13 +406,19 @@
 
 
 def finish(*refs):
-    count = len(refs) // 2
-    copies = [
-        pltpu.make_async_copy(refs[q], refs[count + q], refs[-1].at[q]) for q in range(count)
-    ]
-    for copy in copies:
+    count = (len(refs) - 1) // 3
+    sem = refs[-1]
+    loads, stores = [], []
+    for q in range(count):
+        held = refs[2 * count + q]
+        loads.append(pltpu.make_async_copy(refs[q], held, sem.at[q]))
+        stores.append(pltpu.make_async_copy(held, refs[count + q], sem.at[count + q]))
+    for copy in loads:
         copy.start()
-    for copy in copies:
+    for load, store in zip(loads, stores):
+        load.wait()
+        store.start()
+    for copy in stores:
         copy.wait()
 
 
@@ -485,7 +495,8 @@
         out_shape=results,
         in_specs=[anywhere] * 4,
         out_specs=(anywhere,) * 4,
-        scratch_shapes=[pltpu.SemaphoreType.DMA((4,))],
+        scratch_shapes=[pltpu.VMEM(result.shape, result.dtype) for result in results]
+        + [pltpu.SemaphoreType.DMA((8,))],
     )(*found)
     return (
         forces.reshape(positions.shape),

time: 23.7 us -> 22.1 us (0.932)
  Pallas kernels: 22.9 us -> 21.2 us
    pallas_call x1, Pallas kernels: 3.22 us -> 1.55 us  [shards(): pl.pallas_call(finish, out_shape=results, in_specs=[anywhere] * 4, out_sp...]
where the time goes in v3:
time: 22.1 us; the launch traced here: 21.9 us
  Pallas kernels  21.2 us (96%)
  between operations  0.64 us (3%)
    pallas_call x1, Pallas kernels, shards(): pl.pallas_call(functools.partial(kernel, axes), out_shape=results, in_spe...  19.7 us
    pallas_call x1, Pallas kernels, shards(): pl.pallas_call(finish, out_shape=results, in_specs=[anywhere] * 4, out_sp...  1.55 us

profile of v3, /device:TPU:0, one launch (start us, length us, event | category | flops | bytes accessed | tf_op | source)
XLA Modules:
  0.0 21.9 jit_solution(7528458404514921407)
XLA Ops:
  0.6 19.7 %shard_map.156 = (f32[3,1,64]{2,1,0:T(1,128)}, f32[1,64]{1,0:T(1,128)}, bf16[3,64]{1,0:T(4,128)(2,1)}, bf16[64,512]{1,0:T(8,128)(2,1)}) custom-call(bf16[3,64]{1,0:T(4,128)(2,1)} %bitcast.19, bf16[64,512]{1,0:T(8,128)(2,1)} %bitcast.13, s32[3,2,48]{2,1,0:T(2,128)} %bitcast.16, s32[3,2,4]{2,1,0:T(2,128)} %bitcast.17, s32[8,64]{1,0:T(8,128)} %bitcast.15, ...), custom_call_target="tpu_custom_call" | custom-call | tf_op jit(solution)/shard_map/pallas_call | solution.py:467
  20.3 1.6 %shard_map.157 = (f32[3,1,64]{2,1,0:T(1,128)}, f32[1,64]{1,0:T(1,128)}, bf16[3,64]{1,0:T(4,128)(2,1)}, bf16[64,512]{1,0:T(8,128)(2,1)}) custom-call(f32[3,1,64]{2,1,0:T(1,128)} %get-tuple-element.12.refs_0_, f32[1,64]{1,0:T(1,128)} %get-tuple-element.13.refs_1_, bf16[3,64]{1,0:T(4,128)(2,1)} %get-tuple-element.14.refs_2_, ...), custom_call_target="tpu_custom_call" | custom-call | tf_op jit(solution)/shard_map/pallas_call | solution.py:493
